TPU v7x, 32 devices: a whole 2x2x4 slice. The times are simulated.
32 devices in a mesh: dp: 8 (over z, y), head: 4 (over x, core).
Axes of the slice: x: 2, y: 2, z: 4, core: 2. Of those that a mesh axis runs over, the one named last changes fastest.
Arguments:
- queries: bfloat16 [8192, 4096], P('dp', 'head'), may hold values from -6 to 6
- keys: bfloat16 [8192, 4096], P('dp', 'head'), may hold values from -6 to 6
- values: bfloat16 [8192, 4096], P('dp', 'head'), may hold values from -100 to 100
- out_grad: bfloat16 [8192, 4096], P('dp', 'head'), may hold values from -6 to 6
- norm_gain: float32 [4096], P('head'), may hold values from 0.1 to 1.9
- decay_table: float32 [16, 8], P('head'), may hold values from 0 to 0.52, as said below
- decay_index: int32 [16, 8192], P('head', 'dp'), may hold values from 0 to 7
- rollout_lengths: int32 [6], replicated, may hold values from 1 to 4096, 8192 in all
- move_partner: int32 [8], replicated, may hold values from 0 to 7, as said below
- move_slot: int32 [8], replicated, may hold values from 0 to 31, as said below
Outputs:
- query_grad: bfloat16 [8192, 4096], P('dp', 'head')
- key_grad: bfloat16 [8192, 4096], P('dp', 'head')
- value_grad: bfloat16 [8192, 4096], P('dp', 'head')
Inputs may be any that keep to these rules, and one draw needn't show every extreme that they name: `decay_table`: positive rates. `rollout_lengths`: they sum to 8192. move_partner[d] is either d itself or a row whose index differs from d in exactly one bit, and the partner of the partner is the row itself. `move_slot`: one block of each row.
All inputs are finite; a program needn't handle non-finite values.
Results may differ from a plain program's by a relative error of at most 0.0063.
Values may be sent and summed in bfloat16 or wider, within the bound.
A program may use at most 128 MiB of HBM per device.

v0:
```python
import jax
import jax.numpy as jnp
from jax import lax
from jax.sharding import PartitionSpec as P

HEAD_DIM = 256
BLOCK_LEN = 32
FEATURES = 4096


EPSILON = 1e-05


def partner_2(block, axis, apart):
    count = lax.axis_size(axis)
    route = []
    for low in range(count):
        high = low | 1 << apart
        if high != low and high < count:
            route += [(low, high), (high, low)]
    return lax.ppermute(block, axis, route)


def entering(part, axis, combine, identity, reverse):
    count = lax.axis_size(axis)
    place = lax.axis_index(axis)
    ahead = count - 1 - place if reverse else place
    gathered = jax.tree.map(lambda a: lax.all_gather(a, axis), part)
    state = jax.tree.map(lambda a, e: jnp.zeros_like(a) + jnp.asarray(e, a.dtype), part, identity)

    def one(turn, state):
        source = count - 1 - turn if reverse else turn
        return combine(
            state, jax.tree.map(lambda a: lax.dynamic_index_in_dim(a, source, 0, False), gathered)
        )

    return lax.fori_loop(0, ahead, one, state)


def shortened(value):

    def short(part):
        return part.astype(jnp.bfloat16) if part.dtype == jnp.float32 else part

    return jax.tree.map(short, value)


def edge_factors(rate, flag):
    segment = jnp.cumsum(flag.astype(jnp.int32))
    total = jnp.cumsum(rate, axis=1)
    first = jnp.where(segment[None, :] == 0, jnp.exp(-total), 0.0)
    last = jnp.where(segment[None, :] == segment[-1], jnp.exp(total - total[:, -1:]), 0.0)
    whole = jnp.where(segment[-1] == 0, jnp.exp(-total[:, -1]), 0.0)
    return (total, segment, first, last, whole)


def decay_matrix(total_row, segment):
    count = segment.shape[0]
    places = jnp.arange(count)
    inside = (segment[:, None] == segment[None, :]) & (places[:, None] >= places[None, :])
    return jnp.where(
        inside, jnp.exp(jnp.minimum(total_row[None, :] - total_row[:, None], 0.0)), 0.0
    )


def combine_states(before, behind):
    return (before[0] * behind[0], behind[0][:, None, None] * before[1] + behind[1])


def take_block(array, block_id, length, axis_dim):
    return lax.dynamic_slice_in_dim(array, block_id * length, length, axis_dim)


def place_block(array, block, block_id, axis_dim):
    return lax.dynamic_update_slice_in_dim(array, block, block_id * block.shape[axis_dim], axis_dim)


def contract_first(left, right):
    return lax.dot_general(
        left, right, (((0,), (0,)), ((), ())), preferred_element_type=jnp.float32
    )


def contract_last(left, right):
    return lax.dot_general(
        left, right, (((1,), (1,)), ((), ())), preferred_element_type=jnp.float32
    )


def local(
    queries,
    keys,
    values,
    out_grad,
    norm_gain,
    decay_table,
    decay_index,
    rollout_lengths,
    move_partner,
    move_slot,
):
    row_index = lax.axis_index("dp")
    row_count = lax.axis_size("dp")
    row_tokens = queries.shape[0]
    heads_here = decay_table.shape[0]
    length = BLOCK_LEN
    partner = move_partner[row_index]
    own_slot = move_slot[row_index]
    bit_count = row_count.bit_length() - 1
    outgoing = (
        take_block(queries, own_slot, length, 0),
        take_block(keys, own_slot, length, 0),
        take_block(values, own_slot, length, 0),
        take_block(out_grad, own_slot, length, 0),
        take_block(decay_index, own_slot, length, 1),
    )
    guest = outgoing
    for level in range(bit_count):
        swapped = partner_2(
            (outgoing[0], outgoing[1], outgoing[2], outgoing[3], outgoing[4]), "dp", level
        )
        matches = partner == jnp.bitwise_xor(row_index, 1 << level)
        guest = tuple((jnp.where(matches, fresh, kept) for fresh, kept in zip(swapped, guest)))
    packed_q = place_block(queries, guest[0], own_slot, 0)
    packed_k = place_block(keys, guest[1], own_slot, 0)
    packed_v = place_block(values, guest[2], own_slot, 0)
    packed_dy = place_block(out_grad, guest[3], own_slot, 0)
    packed_index = place_block(decay_index, guest[4], own_slot, 1)
    level_ids = jnp.arange(decay_table.shape[1], dtype=jnp.int32)
    rate = jnp.sum(
        jnp.where(packed_index[:, :, None] == level_ids, decay_table[:, None, :], 0.0), axis=2
    )
    starts = jnp.cumsum(rollout_lengths) - rollout_lengths
    position = row_index * row_tokens + jnp.arange(row_tokens, dtype=jnp.int32)
    flag = jnp.any(position[:, None] == starts[None, :], axis=1)
    total, segment, first, last, whole = edge_factors(rate, flag)
    head_cols = []
    local_states = []
    for head_pos in range(heads_here):
        columns = slice(head_pos * HEAD_DIM, (head_pos + 1) * HEAD_DIM)
        head_cols.append(columns)
        gated_values = (packed_v[:, columns].astype(jnp.float32) * last[head_pos][:, None]).astype(
            jnp.bfloat16
        )
        local_states.append(contract_first(packed_k[:, columns], gated_values))
    stacked = jnp.stack(local_states)
    identity = (jnp.ones_like(whole), jnp.zeros_like(stacked))
    _, carry_in = entering((whole, stacked), "dp", combine_states, identity, False)
    carry_half = carry_in.astype(jnp.bfloat16)
    decays = []
    weight_list = []
    retained_parts = []
    for head_pos in range(heads_here):
        columns = head_cols[head_pos]
        query_head = packed_q[:, columns]
        decay = decay_matrix(total[head_pos], segment)
        scores = contract_last(query_head, packed_k[:, columns])
        weights = (scores * decay / HEAD_DIM).astype(jnp.bfloat16)
        inner_part = jnp.dot(weights, packed_v[:, columns], preferred_element_type=jnp.float32)
        cross_part = (
            first[head_pos][:, None]
            * jnp.dot(query_head, carry_half[head_pos], preferred_element_type=jnp.float32)
            / HEAD_DIM
        )
        decays.append(decay)
        weight_list.append(weights)
        retained_parts.append(inner_part + cross_part)
    retained = jnp.concatenate(retained_parts, axis=1)
    scaled = norm_gain * packed_dy.astype(jnp.float32)
    squares, inner = lax.psum(
        (jnp.sum(retained * retained, axis=1), jnp.sum(scaled * retained, axis=1)), "head"
    )
    recip = lax.rsqrt(squares / FEATURES + EPSILON)
    norm_grad = (
        recip[:, None] * scaled - (recip**3 * inner / FEATURES)[:, None] * retained
    ).astype(jnp.bfloat16)
    back_locals = []
    for head_pos in range(heads_here):
        columns = head_cols[head_pos]
        weighted = (norm_grad[:, columns].astype(jnp.float32) * first[head_pos][:, None]).astype(
            jnp.bfloat16
        )
        back_locals.append(contract_first(packed_q[:, columns], weighted) / HEAD_DIM)
    back_stack = jnp.stack(back_locals)
    _, carry_back = entering(
        (whole, back_stack),
        "dp",
        combine_states,
        (jnp.ones_like(whole), jnp.zeros_like(back_stack)),
        True,
    )
    back_half = carry_back.astype(jnp.bfloat16)
    query_parts = []
    key_parts = []
    value_parts = []
    for head_pos in range(heads_here):
        columns = head_cols[head_pos]
        query_head = packed_q[:, columns]
        key_head = packed_k[:, columns]
        value_head = packed_v[:, columns]
        grad_head = norm_grad[:, columns]
        grad_scores = contract_last(grad_head, value_head)
        grad_weights = (grad_scores * decays[head_pos] / HEAD_DIM).astype(jnp.bfloat16)
        query_part = jnp.dot(grad_weights, key_head, preferred_element_type=jnp.float32)
        query_part = (
            query_part
            + first[head_pos][:, None] * contract_last(grad_head, carry_half[head_pos]) / HEAD_DIM
        )
        key_part = contract_first(grad_weights, query_head)
        key_part = key_part + last[head_pos][:, None] * contract_last(
            value_head, back_half[head_pos]
        )
        value_part = contract_first(weight_list[head_pos], grad_head)
        value_part = value_part + last[head_pos][:, None] * jnp.dot(
            key_head, back_half[head_pos], preferred_element_type=jnp.float32
        )
        query_parts.append(query_part)
        key_parts.append(key_part)
        value_parts.append(value_part)
    packed_grads = (
        jnp.concatenate(query_parts, axis=1).astype(jnp.bfloat16),
        jnp.concatenate(key_parts, axis=1).astype(jnp.bfloat16),
        jnp.concatenate(value_parts, axis=1).astype(jnp.bfloat16),
    )
    leaving = tuple((take_block(member, own_slot, length, 0) for member in packed_grads))
    returned = leaving
    for level in range(bit_count):
        swapped_back = jax.tree.map(
            lambda part, own: part.astype(own.dtype),
            partner_2(shortened(leaving), "dp", level),
            leaving,
        )
        matches = partner == jnp.bitwise_xor(row_index, 1 << level)
        returned = tuple(
            (jnp.where(matches, fresh, kept) for fresh, kept in zip(swapped_back, returned))
        )
    query_grad = place_block(packed_grads[0], returned[0], own_slot, 0)
    key_grad = place_block(packed_grads[1], returned[1], own_slot, 0)
    value_grad = place_block(packed_grads[2], returned[2], own_slot, 0)
    return (query_grad, key_grad, value_grad)


def solution(mesh):
    placed = (
        P("dp", "head"),
        P("dp", "head"),
        P("dp", "head"),
        P("dp", "head"),
        P("head"),
        P("head", None),
        P("head", "dp"),
        P(),
        P(),
        P(),
    )
    return jax.shard_map(
        local,
        mesh=mesh,
        in_specs=placed,
        out_specs=(P("dp", "head"), P("dp", "head"), P("dp", "head")),
        check_vma=False,
    )
```

profile of v0, /device:TPU:0, one launch (start us, length us, event | category | flops | bytes accessed | tf_op | source)
XLA Modules:
  0.0 435.6 jit_solution(1993645834230065091)
XLA Ops:
  7.9 3.2 copy.100
  13.8 3.0 collective-permute-start.8
  16.8 1.6 collective-permute-start.7
  18.4 2.6 collective-permute-start.6
  21.0 2.9 copy.54
  32.4 1.8 collective-permute-start.2
  34.2 1.6 collective-permute-start.1
  38.1 2.7 collective-permute-start
  41.3 9.0 %collective-permute-done.9 = bf16[32,1024]{0,1:T(8,128)(2,1)S(1)} collective-permute-done((bf16[32,1024]{0,1:T(8,128)(2,1)}, bf16[32,1024]{0,1:T(8,128)(2,1)S(1)}, u32[]{:S(2)}, u32[]{:S(2)}) %collective-permute-start.9) | collective-permute-done | bytes 65568 | tf_op jit(solution)/shard_map/ppermute | solution.py:21
  51.3 2.0 dynamic_update_slice.29
  53.3 10.6 %collective-permute-done = bf16[32,1024]{0,1:T(8,128)(2,1)} collective-permute-done((bf16[32,1024]{0,1:T(8,128)(2,1)S(1)}, bf16[32,1024]{0,1:T(8,128)(2,1)}, u32[]{:S(2)}, u32[]{:S(2)}) %collective-permute-start) | collective-permute-done | bytes 65568 | tf_op jit(solution)/shard_map/ppermute | solution.py:21
  63.9 4.4 %collective-permute-done.3 = bf16[32,1024]{0,1:T(8,128)(2,1)} collective-permute-done((bf16[32,1024]{0,1:T(8,128)(2,1)S(1)}, bf16[32,1024]{0,1:T(8,128)(2,1)}, u32[]{:S(2)}, u32[]{:S(2)}) %collective-permute-start.3) | collective-permute-done | bytes 65568 | tf_op jit(solution)/shard_map/ppermute | solution.py:21
  70.2 1.5 convolution_bitcast_fusion.3
  75.1 2.9 copy.57
  78.1 1.7 collective-permute-start.14
  79.8 1.7 collective-permute-start.12
  83.4 30.7 %all-reduce = f32[32]{0:T(128)S(1)} all-reduce(f32[32]{0:T(128)S(1)} %fusion.100), channel_id=2, replica_groups=mesh['dp'=8,'head'=4] {'dp'}, use_global_device_ids=true, to_apply=%add | all-reduce | flops 32 | bytes 256
  114.5 2.0 dynamic_update_slice.30
  117.3 3.9 multiply_convert_fusion.4
  121.2 3.1 multiply_convert_fusion.5
  124.3 3.2 multiply_convert_fusion.6
  127.5 3.1 multiply_convert_fusion.7
  130.5 75.4 %all-gather.6.cloned.1.call-done = f32[32,256,256]{2,1,0:T(8,128)} async-done(((f32[4,256,256]{2,1,0:T(8,128)}), f32[32,256,256]{2,1,0:T(8,128)}) %all-gather.6.cloned.1.call-update) | async-done | bytes 8388624 | tf_op jit(solution)/shard_map/all_gather | solution.py:28
  206.1 1.6 fusion.5
  216.4 3.2 multiply_reduce_fusion.1
  219.6 6.5 %all-reduce.1 = (f32[1024]{0:T(1024)S(1)}, f32[1024]{0:T(1024)S(1)}) all-reduce(f32[1024]{0:T(1024)S(1)} %get-tuple-element.146, f32[1024]{0:T(1024)S(1)} %get-tuple-element.145), channel_id=1, replica_groups=mesh['dp'=8,'head'=4] {'head'}, use_global_device_ids=true, to_apply=%region_12.13 | all-reduce | flops 2048 | bytes 16384 | tf_op jit(solution)/shard_map/psum | solution.py:170
  226.1 2.4 subtract_convert_fusion
  235.6 2.2 multiply_convert_fusion
  239.2 2.2 multiply_convert_fusion.1
  242.8 2.3 multiply_convert_fusion.2
  245.9 2.3 multiply_convert_fusion.3
  252.0 2.1 collective-permute-start.17
  254.1 2.7 collective-permute-start.16
  256.7 9.0 %collective-permute-start.15 = (bf16[32,1024]{0,1:T(8,128)(2,1)S(1)}, bf16[32,1024]{0,1:T(8,128)(2,1)S(1)}, u32[]{:S(2)}, u32[]{:S(2)}) collective-permute-start(bf16[32,1024]{0,1:T(8,128)(2,1)S(1)} %constant_dynamic-slice_fusion.2), channel_id=1, source_target_pairs={{0,16},{16,0},{4,20},{20,4},{8,24},{24,8},{12,28},{28,12},{1,17},{... | collective-permute-start | bytes 196616 | tf_op jit(solution)/shard_map/ppermute | solution.py:21
  266.4 16.2 %collective-permute-done.16 = bf16[32,1024]{0,1:T(8,128)(2,1)S(1)} collective-permute-done((bf16[32,1024]{0,1:T(8,128)(2,1)S(1)}, bf16[32,1024]{0,1:T(8,128)(2,1)S(1)}, u32[]{:S(2)}, u32[]{:S(2)}) %collective-permute-start.16) | collective-permute-done | bytes 65568 | tf_op jit(solution)/shard_map/ppermute | solution.py:21
  282.6 6.9 %collective-permute-done.15 = bf16[32,1024]{0,1:T(8,128)(2,1)S(1)} collective-permute-done((bf16[32,1024]{0,1:T(8,128)(2,1)S(1)}, bf16[32,1024]{0,1:T(8,128)(2,1)S(1)}, u32[]{:S(2)}, u32[]{:S(2)}) %collective-permute-start.15) | collective-permute-done | bytes 65568 | tf_op jit(solution)/shard_map/ppermute | solution.py:21
  290.6 3.9 dynamic_update_slice.31
  294.5 3.9 copy.58
  298.4 77.7 %all-gather.8.cloned.1.call-done = f32[32,256,256]{2,1,0:T(8,128)} async-done(((f32[4,256,256]{2,1,0:T(8,128)}), f32[32,256,256]{2,1,0:T(8,128)}) %all-gather.8.cloned.1.call-update) | async-done | bytes 8388624 | tf_op jit(solution)/shard_map/all_gather | solution.py:28
  376.2 10.8 %while.27 = (s32[]{:T(128)}, f32[4,256,256]{2,1,0:T(8,128)S(1)}, s32[]{:T(128)}, f32[8,4]{1,0:T(8,128)S(1)}, f32[8,4,256,256]{3,2,1,0:T(8,128)}, /*index=5*/s32[]{:T(128)}, s32[]{:T(128)}, s32[]{:T(128)}, s32[]{:T(128)}) while((s32[]{:T(128)}, f32[4,256,256]{2,1,0:T(8,128)S(1)}, s32[]{:T(128)}, f32[8,4]{1,0:T(8,128)S(1)}, ...), condition=%wide.region_14.15_spmd, body=%wide.region_13.14_spmd.sunk | while | flops 524294 | bytes 3145931 | solution.py:37
  387.1 1.5 convolution_multiply_fusion.8
  406.4 1.8 collective-permute-start.19
  408.2 2.9 collective-permute-start.18
  411.1 3.0 collective-permute-done.21
  414.3 3.8 dynamic_update_slice.33
  418.1 3.9 copy.60
  423.7 2.0 dynamic_update_slice.32
  425.8 2.6 copy.59
  (242 shorter events, 74.9 us)
Async XLA Ops:
  7.2 198.8 %all-gather.6.cloned.1.call-start = ((), (), s32[]{:S(2)}) async-start(), calls=%async_computation | async-start | bytes 9437184 | tf_op jit(solution)/shard_map/all_gather | solution.py:28
  7.9 3.2 copy-start.30
  13.8 11.8 %copy-start.43 = (s32[6]{0:T(128)S(1)}, s32[6]{0:T(128)}, u32[]{:S(2)}) copy-start(s32[6]{0:T(128)} %param.21) | copy-start | bytes 76
  13.8 15.6 %copy-start.44 = (s32[8]{0:T(128)S(1)}, s32[8]{0:T(128)}, u32[]{:S(2)}) copy-start(s32[8]{0:T(128)} %param.22) | copy-start | bytes 100
  13.8 22.3 %copy-start.41 = (f32[4,8]{1,0:T(4,128)S(1)}, f32[4,8]{1,0:T(4,128)}, u32[]{:S(2)}) copy-start(f32[4,8]{1,0:T(4,128)} %param.19) | copy-start | bytes 388
  13.8 18.5 %collective-permute-start.8 = (s32[4,32]{1,0:T(4,128)S(1)}, s32[4,32]{1,0:T(4,128)S(1)}, u32[]{:S(2)}, u32[]{:S(2)}) collective-permute-start(s32[4,32]{1,0:T(4,128)S(1)} %constant_dynamic-slice_fusion.5), channel_id=1, source_target_pairs={{0,4},{4,0},{8,12},{12,8},{16,20},{20,16},{24,28},{28,24},{1,5},{5... | collective-permute-start | bytes 1544 | tf_op jit(solution)/shard_map/ppermute | solution.py:21
  16.8 15.6 %collective-permute-start.7 = (s32[4,32]{1,0:T(4,128)S(1)}, s32[4,32]{1,0:T(4,128)S(1)}, u32[]{:S(2)}, u32[]{:S(2)}) collective-permute-start(s32[4,32]{1,0:T(4,128)S(1)} %constant_dynamic-slice_fusion.5), channel_id=1, source_target_pairs={{0,8},{8,0},{4,12},{12,4},{16,24},{24,16},{20,28},{28,20},{1,9},{9... | collective-permute-start | bytes 1544 | tf_op jit(solution)/shard_map/ppermute | solution.py:21
  18.4 15.8 %collective-permute-start.6 = (s32[4,32]{1,0:T(4,128)S(1)}, s32[4,32]{1,0:T(4,128)S(1)}, u32[]{:S(2)}, u32[]{:S(2)}) collective-permute-start(s32[4,32]{1,0:T(4,128)S(1)} %constant_dynamic-slice_fusion.5), channel_id=1, source_target_pairs={{0,16},{16,0},{4,20},{20,4},{8,24},{24,8},{12,28},{28,12},{1,17},{... | collective-permute-start | bytes 1544 | tf_op jit(solution)/shard_map/ppermute | solution.py:21
  24.7 13.4 %collective-permute-start.11 = (bf16[32,1024]{0,1:T(8,128)(2,1)}, bf16[32,1024]{0,1:T(8,128)(2,1)S(1)}, u32[]{:S(2)}, u32[]{:S(2)}) collective-permute-start(bf16[32,1024]{0,1:T(8,128)(2,1)} %constant_dynamic-slice_fusion.4), channel_id=1, source_target_pairs={{0,4},{4,0},{8,12},{12,8},{16,20},{20,16},{24,28},{28,24},{1,5},{5... | collective-permute-start | bytes 196616 | tf_op jit(solution)/shard_map/ppermute | solution.py:21
  25.2 15.6 %collective-permute-start.10 = (bf16[32,1024]{0,1:T(8,128)(2,1)}, bf16[32,1024]{0,1:T(8,128)(2,1)S(1)}, u32[]{:S(2)}, u32[]{:S(2)}) collective-permute-start(bf16[32,1024]{0,1:T(8,128)(2,1)} %constant_dynamic-slice_fusion.4), channel_id=1, source_target_pairs={{0,8},{8,0},{4,12},{12,4},{16,24},{24,16},{20,28},{28,20},{1,9},{9... | collective-permute-start | bytes 196616 | tf_op jit(solution)/shard_map/ppermute | solution.py:21
  32.3 18.0 %collective-permute-start.9 = (bf16[32,1024]{0,1:T(8,128)(2,1)}, bf16[32,1024]{0,1:T(8,128)(2,1)S(1)}, u32[]{:S(2)}, u32[]{:S(2)}) collective-permute-start(bf16[32,1024]{0,1:T(8,128)(2,1)} %constant_dynamic-slice_fusion.4), channel_id=1, source_target_pairs={{0,16},{16,0},{4,20},{20,4},{8,24},{24,8},{12,28},{28,12},{1,17},{... | collective-permute-start | bytes 196616 | tf_op jit(solution)/shard_map/ppermute | solution.py:21
  32.4 17.9 %collective-permute-start.2 = (bf16[32,1024]{0,1:T(8,128)(2,1)S(1)}, bf16[32,1024]{0,1:T(8,128)(2,1)}, u32[]{:S(2)}, u32[]{:S(2)}) collective-permute-start(bf16[32,1024]{0,1:T(8,128)(2,1)S(1)} %copy.61), channel_id=1, source_target_pairs={{0,4},{4,0},{8,12},{12,8},{16,20},{20,16},{24,28},{28,24},{1,5},{5... | collective-permute-start | bytes 196616 | tf_op jit(solution)/shard_map/ppermute | solution.py:21
  34.2 19.1 %collective-permute-start.1 = (bf16[32,1024]{0,1:T(8,128)(2,1)S(1)}, bf16[32,1024]{0,1:T(8,128)(2,1)}, u32[]{:S(2)}, u32[]{:S(2)}) collective-permute-start(bf16[32,1024]{0,1:T(8,128)(2,1)S(1)} %copy.61), channel_id=1, source_target_pairs={{0,8},{8,0},{4,12},{12,4},{16,24},{24,16},{20,28},{28,20},{1,9},{9... | collective-permute-start | bytes 196616 | tf_op jit(solution)/shard_map/ppermute | solution.py:21
  38.1 25.8 %collective-permute-start = (bf16[32,1024]{0,1:T(8,128)(2,1)S(1)}, bf16[32,1024]{0,1:T(8,128)(2,1)}, u32[]{:S(2)}, u32[]{:S(2)}) collective-permute-start(bf16[32,1024]{0,1:T(8,128)(2,1)S(1)} %copy.61), channel_id=1, source_target_pairs={{0,16},{16,0},{4,20},{20,4},{8,24},{24,8},{12,28},{28,12},{1,17},{... | collective-permute-start | bytes 196616 | tf_op jit(solution)/shard_map/ppermute | solution.py:21
  40.8 23.1 %collective-permute-start.5 = (bf16[32,1024]{0,1:T(8,128)(2,1)S(1)}, bf16[32,1024]{0,1:T(8,128)(2,1)}, u32[]{:S(2)}, u32[]{:S(2)}) collective-permute-start(bf16[32,1024]{0,1:T(8,128)(2,1)S(1)} %copy.62), channel_id=1, source_target_pairs={{0,4},{4,0},{8,12},{12,8},{16,20},{20,16},{24,28},{28,24},{1,5},{5... | collective-permute-start | bytes 196616 | tf_op jit(solution)/shard_map/ppermute | solution.py:21
  50.3 13.6 %collective-permute-start.4 = (bf16[32,1024]{0,1:T(8,128)(2,1)S(1)}, bf16[32,1024]{0,1:T(8,128)(2,1)}, u32[]{:S(2)}, u32[]{:S(2)}) collective-permute-start(bf16[32,1024]{0,1:T(8,128)(2,1)S(1)} %copy.62), channel_id=1, source_target_pairs={{0,8},{8,0},{4,12},{12,4},{16,24},{24,16},{20,28},{28,20},{1,9},{9... | collective-permute-start | bytes 196616 | tf_op jit(solution)/shard_map/ppermute | solution.py:21
  51.0 17.3 %collective-permute-start.3 = (bf16[32,1024]{0,1:T(8,128)(2,1)S(1)}, bf16[32,1024]{0,1:T(8,128)(2,1)}, u32[]{:S(2)}, u32[]{:S(2)}) collective-permute-start(bf16[32,1024]{0,1:T(8,128)(2,1)S(1)} %copy.62), channel_id=1, source_target_pairs={{0,16},{16,0},{4,20},{20,4},{8,24},{24,8},{12,28},{28,12},{1,17},{... | collective-permute-start | bytes 196616 | tf_op jit(solution)/shard_map/ppermute | solution.py:21
  53.3 20.3 %copy-start = (bf16[1024,1024]{0,1:T(8,128)(2,1)}, bf16[1024,1024]{0,1:T(8,128)(2,1)S(1)}, u32[]{:S(2)}) copy-start(bf16[1024,1024]{0,1:T(8,128)(2,1)S(1)} %dynamic_update_slice.29) | copy-start | bytes 6291460
  70.2 3.0 copy-start.3
  75.0 7.0 %copy-start.45 = (u32[32]{0:T(128)S(1)}, u32[32]{0:T(128)}, u32[]{:S(2)}) copy-start(u32[32]{0:T(128)} %constant.121) | copy-start | bytes 388
  75.1 301.1 %all-gather.8.cloned.1.call-start = ((), (), s32[]{:S(2)}) async-start(), calls=%async_computation.1 | async-start | bytes 9437184 | tf_op jit(solution)/shard_map/all_gather | solution.py:28
  78.1 36.1 %collective-permute-start.14 = (bf16[32,1024]{0,1:T(8,128)(2,1)S(1)}, bf16[32,1024]{0,1:T(8,128)(2,1)S(1)}, u32[]{:S(2)}, u32[]{:S(2)}) collective-permute-start(bf16[32,1024]{0,1:T(8,128)(2,1)S(1)} %constant_dynamic-slice_fusion.3), channel_id=1, source_target_pairs={{0,4},{4,0},{8,12},{12,8},{16,20},{20,16},{24,28},{28,24},{1,5},{5... | collective-permute-start | bytes 196616 | tf_op jit(solution)/shard_map/ppermute | solution.py:21
  79.8 34.4 %collective-permute-start.13 = (bf16[32,1024]{0,1:T(8,128)(2,1)S(1)}, bf16[32,1024]{0,1:T(8,128)(2,1)S(1)}, u32[]{:S(2)}, u32[]{:S(2)}) collective-permute-start(bf16[32,1024]{0,1:T(8,128)(2,1)S(1)} %constant_dynamic-slice_fusion.3), channel_id=1, source_target_pairs={{0,8},{8,0},{4,12},{12,4},{16,24},{24,16},{20,28},{28,20},{1,9},{9... | collective-permute-start | bytes 196616 | tf_op jit(solution)/shard_map/ppermute | solution.py:21
  79.8 34.4 %collective-permute-start.12 = (bf16[32,1024]{0,1:T(8,128)(2,1)S(1)}, bf16[32,1024]{0,1:T(8,128)(2,1)S(1)}, u32[]{:S(2)}, u32[]{:S(2)}) collective-permute-start(bf16[32,1024]{0,1:T(8,128)(2,1)S(1)} %constant_dynamic-slice_fusion.3), channel_id=1, source_target_pairs={{0,16},{16,0},{4,20},{20,4},{8,24},{24,8},{12,28},{28,12},{1,17},{... | collective-permute-start | bytes 196616 | tf_op jit(solution)/shard_map/ppermute | solution.py:21
  117.2 3.9 copy-start.4
  117.2 3.9 copy-start.24
  206.0 1.9 copy-start.25
  206.1 2.6 copy-start.28
  208.3 2.0 copy-start.1
  213.5 2.7 copy-start.19
  213.5 2.0 copy-start.11
  216.4 3.2 copy-start.21
  226.1 2.5 copy-start.26
  230.4 2.0 copy-start.8
  235.6 2.3 copy-start.5
  245.1 3.0 copy-start.31
  252.0 14.4 %collective-permute-start.17 = (bf16[32,1024]{0,1:T(8,128)(2,1)S(1)}, bf16[32,1024]{0,1:T(8,128)(2,1)S(1)}, u32[]{:S(2)}, u32[]{:S(2)}) collective-permute-start(bf16[32,1024]{0,1:T(8,128)(2,1)S(1)} %constant_dynamic-slice_fusion.2), channel_id=1, source_target_pairs={{0,4},{4,0},{8,12},{12,8},{16,20},{20,16},{24,28},{28,24},{1,5},{5... | collective-permute-start | bytes 196616 | tf_op jit(solution)/shard_map/ppermute | solution.py:21
  254.1 28.5 %collective-permute-start.16 = (bf16[32,1024]{0,1:T(8,128)(2,1)S(1)}, bf16[32,1024]{0,1:T(8,128)(2,1)S(1)}, u32[]{:S(2)}, u32[]{:S(2)}) collective-permute-start(bf16[32,1024]{0,1:T(8,128)(2,1)S(1)} %constant_dynamic-slice_fusion.2), channel_id=1, source_target_pairs={{0,8},{8,0},{4,12},{12,4},{16,24},{24,16},{20,28},{28,20},{1,9},{9... | collective-permute-start | bytes 196616 | tf_op jit(solution)/shard_map/ppermute | solution.py:21
  256.7 32.7 %collective-permute-start.15 = (bf16[32,1024]{0,1:T(8,128)(2,1)S(1)}, bf16[32,1024]{0,1:T(8,128)(2,1)S(1)}, u32[]{:S(2)}, u32[]{:S(2)}) collective-permute-start(bf16[32,1024]{0,1:T(8,128)(2,1)S(1)} %constant_dynamic-slice_fusion.2), channel_id=1, source_target_pairs={{0,16},{16,0},{4,20},{20,4},{8,24},{24,8},{12,28},{28,12},{1,17},{... | collective-permute-start | bytes 196616 | tf_op jit(solution)/shard_map/ppermute | solution.py:21
  397.4 2.3 copy-start.34
  397.6 16.5 %copy-start.22 = (bf16[1024,1024]{0,1:T(8,128)(2,1)}, bf16[1024,1024]{0,1:T(8,128)(2,1)S(1)}, u32[]{:S(2)}) copy-start(bf16[1024,1024]{0,1:T(8,128)(2,1)S(1)} %pad_maximum_fusion.3) | copy-start | bytes 6291460
  397.6 2.8 copy-start.27
  397.8 10.4 %collective-permute-start.23 = (bf16[32,1024]{0,1:T(8,128)(2,1)S(1)}, bf16[32,1024]{0,1:T(8,128)(2,1)S(1)}, u32[]{:S(2)}, u32[]{:S(2)}) collective-permute-start(bf16[32,1024]{0,1:T(8,128)(2,1)S(1)} %constant_dynamic-slice_fusion), channel_id=1, source_target_pairs={{0,4},{4,0},{8,12},{12,8},{16,20},{20,16},{24,28},{28,24},{1,5},{5... | collective-permute-start | bytes 196616 | tf_op jit(solution)/shard_map/ppermute | solution.py:21
  397.9 13.2 %collective-permute-start.22 = (bf16[32,1024]{0,1:T(8,128)(2,1)S(1)}, bf16[32,1024]{0,1:T(8,128)(2,1)S(1)}, u32[]{:S(2)}, u32[]{:S(2)}) collective-permute-start(bf16[32,1024]{0,1:T(8,128)(2,1)S(1)} %constant_dynamic-slice_fusion), channel_id=1, source_target_pairs={{0,8},{8,0},{4,12},{12,4},{16,24},{24,16},{20,28},{28,20},{1,9},{9... | collective-permute-start | bytes 196616 | tf_op jit(solution)/shard_map/ppermute | solution.py:21
  397.9 16.1 %collective-permute-start.21 = (bf16[32,1024]{0,1:T(8,128)(2,1)S(1)}, bf16[32,1024]{0,1:T(8,128)(2,1)S(1)}, u32[]{:S(2)}, u32[]{:S(2)}) collective-permute-start(bf16[32,1024]{0,1:T(8,128)(2,1)S(1)} %constant_dynamic-slice_fusion), channel_id=1, source_target_pairs={{0,16},{16,0},{4,20},{20,4},{8,24},{24,8},{12,28},{28,12},{1,17},{... | collective-permute-start | bytes 196616 | tf_op jit(solution)/shard_map/ppermute | solution.py:21
  406.3 15.8 %collective-permute-start.20 = (bf16[32,1024]{0,1:T(8,128)(2,1)S(1)}, bf16[32,1024]{0,1:T(8,128)(2,1)S(1)}, u32[]{:S(2)}, u32[]{:S(2)}) collective-permute-start(bf16[32,1024]{0,1:T(8,128)(2,1)S(1)} %constant_dynamic-slice_fusion.1), channel_id=1, source_target_pairs={{0,4},{4,0},{8,12},{12,8},{16,20},{20,16},{24,28},{28,24},{1,5},{5... | collective-permute-start | bytes 196616 | tf_op jit(solution)/shard_map/ppermute | solution.py:21
  406.4 15.7 %collective-permute-start.19 = (bf16[32,1024]{0,1:T(8,128)(2,1)S(1)}, bf16[32,1024]{0,1:T(8,128)(2,1)S(1)}, u32[]{:S(2)}, u32[]{:S(2)}) collective-permute-start(bf16[32,1024]{0,1:T(8,128)(2,1)S(1)} %constant_dynamic-slice_fusion.1), channel_id=1, source_target_pairs={{0,8},{8,0},{4,12},{12,4},{16,24},{24,16},{20,28},{28,20},{1,9},{9... | collective-permute-start | bytes 196616 | tf_op jit(solution)/shard_map/ppermute | solution.py:21
  408.2 15.3 %collective-permute-start.18 = (bf16[32,1024]{0,1:T(8,128)(2,1)S(1)}, bf16[32,1024]{0,1:T(8,128)(2,1)S(1)}, u32[]{:S(2)}, u32[]{:S(2)}) collective-permute-start(bf16[32,1024]{0,1:T(8,128)(2,1)S(1)} %constant_dynamic-slice_fusion.1), channel_id=1, source_target_pairs={{0,16},{16,0},{4,20},{20,4},{8,24},{24,8},{12,28},{28,12},{1,17},{... | collective-permute-start | bytes 196616 | tf_op jit(solution)/shard_map/ppermute | solution.py:21
  (24 other events, 35.2 us)
Sparse Core Ops, SparseCore 0:
  75.2 130.7 all-gather.5
  231.6 144.5 all-gather.7
where the time goes:
time: 442 us; the launch traced here: 436 us
  waiting for transfers between devices  205 us (46%)
  local copies, waits for them, and re-layouts  64.6 us (15%)
  matrix products  47 us (11%)
  blocking collectives  37.1 us (8%)
  starting transfers between devices  37 us (8%)
  other arithmetic  25 us (6%)
  between operations  19.1 us (4%)
    all_gather x2, waiting for transfers between devices, entering(): gathered = jax.tree.map(lambda a: lax.all_gather(a, axis), part)  153 us
    ppermute x24, waiting for transfers between devices, partner_2(): return lax.ppermute(block, axis, route)  52.2 us
    unnamed x107, local copies, waits for them, and re-layouts  43.3 us
    ppermute x24, starting transfers between devices, partner_2(): return lax.ppermute(block, axis, route)  37 us
    unnamed x1, blocking collectives  30.7 us
    dot_general x16, matrix products, contract_last(): lax.dot_general(left, right, (((1,), (1,)), ((), ())), preferred_element_...  24.7 us
    dynamic_update_slice x8, local copies, waits for them, and re-layouts, place_block(): lax.dynamic_update_slice_in_dim(array, block, block_id * block.shape[axis...  15.2 us
    dot_general x16, matrix products, contract_first(): lax.dot_general(left, right, (((0,), (0,)), ((), ())), preferred_element_...  11 us
  transfers between devices with their start and end apart: 26, of which 10 were waited for; matrix products, arithmetic and copies ran while one was open for 15% of the time, Pallas kernels for 0%

commit v1 on v0

v1 whole, which is shorter than its diff:
```python
import functools

import jax
import jax.numpy as jnp
from jax import lax
from jax.experimental import pallas as pl
from jax.experimental.pallas import tpu as pltpu
from jax.sharding import PartitionSpec as P

HEAD_DIM = 256
BLOCK_LEN = 32
FEATURES = 4096
EPSILON = 1e-05
TILE = 256
MESH = pl.DeviceIdType.MESH
F32 = jnp.float32
BF16 = jnp.bfloat16


def dot_nt(a, b):
    return lax.dot_general(a, b, (((1,), (1,)), ((), ())), preferred_element_type=F32)


def dot_tn(a, b):
    return lax.dot_general(a, b, (((0,), (0,)), ((), ())), preferred_element_type=F32)


def dot_nn(a, b):
    return jnp.dot(a, b, preferred_element_type=F32)


def twice(col):
    return jnp.concatenate([col, col], axis=1)


def to_column(row, tokens):
    return jnp.transpose(jnp.broadcast_to(row, (128, tokens)))


def main_kernel(
    count, hcount, heads, tokens,
    lengths, partners, slots, table, index, gain, q_hbm, k_hbm, v_hbm, dy_hbm,
    dq_hbm, dk_hbm, dv_hbm, guest_out,
    pq, pk, pv, pdy, wts, decay, gw, ret, dkin, grad, colb, segc, cum_s,
    rate_out, rate_in, blk_out, blk_in, w_in, w_out,
    st_out, st_in, st_ret, carry, bk_in, bk_ret, cback,
    hs_out, hs_in, lv_out, lv_in,
    in_sem, out_sem, rate_ss, rate_rs, blk_ss, blk_rs, w_ss, w_rs,
    p1_ss, p1_rs, p2_ss, p2_rs, b1_ss, b1_rs, b2_ss, b2_rs, hs_ss, hs_rs, lv_ss, lv_rs,
):
    me = lax.axis_index("dp")
    hme = lax.axis_index("head")
    levels = count.bit_length() - 1
    length = BLOCK_LEN
    span = heads * HEAD_DIM // count
    tiles = tokens // TILE
    width = heads * HEAD_DIM
    inv = 1.0 / HEAD_DIM

    loads = []
    for i, (src, dst) in enumerate(((k_hbm, pk), (v_hbm, pv), (q_hbm, pq), (dy_hbm, pdy))):
        copy = pltpu.make_async_copy(src, dst, in_sem.at[i])
        copy.start()
        loads.append(copy)

    barrier = pltpu.get_barrier_semaphore()
    for o in range(1, count):
        pl.semaphore_signal(barrier, inc=1, device_id={"dp": lax.rem(me + o, count)}, device_id_type=MESH)
    for o in range(1, hcount):
        pl.semaphore_signal(barrier, inc=1, device_id={"head": lax.rem(hme + o, hcount)}, device_id_type=MESH)

    idx = index[...]
    rate = jnp.zeros((heads, tokens), F32)
    for level in range(table.shape[1]):
        rate = jnp.where(idx == level, table[:, level:level + 1], rate)
    rate_out[...] = jnp.zeros((8, tokens), F32)
    rate_out[0:heads, :] = rate

    slot = slots[me]
    partner = partners[me]
    partner_slot = slot
    for d in range(count):
        partner_slot = jnp.where(partner == d, slots[d], partner_slot)
    pl.semaphore_wait(barrier, count - 1 + hcount - 1)

    def remote(src, dst, ss, rs, axis, to):
        return pltpu.make_async_remote_copy(
            src_ref=src, dst_ref=dst, send_sem=ss, recv_sem=rs,
            device_id={axis: to}, device_id_type=MESH,
        )

    def other(level):
        bit = 1 << level
        return me + bit - 2 * bit * (lax.rem(me // bit, 2))

    rate_copies = []
    for level in range(levels):
        copy = remote(rate_out, rate_in.at[level], rate_ss.at[level], rate_rs.at[level], "dp", other(level))
        copy.start()
        rate_copies.append(copy)

    blocks = tokens // length

    def pick(ref):
        slot_of = jnp.full((length, width), slot, jnp.int32)

        def one(b, acc):
            part = ref[pl.ds(pl.multiple_of(b * length, length), length), :].astype(F32)
            return jnp.where(slot_of == b, part, acc)

        return lax.fori_loop(0, blocks, one, jnp.zeros((length, width), F32)).astype(BF16)

    for i, ref in enumerate((pk, pv, pq, pdy)):
        loads[i].wait()
        blk_out[i] = pick(ref)
    blk_copies = []
    for level in range(levels):
        copy = remote(blk_out, blk_in.at[level], blk_ss.at[level], blk_rs.at[level], "dp", other(level))
        copy.start()
        blk_copies.append(copy)

    lane = lax.broadcasted_iota(jnp.int32, (8, tokens), 1)
    sub = lax.broadcasted_iota(jnp.int32, (8, tokens), 0)
    flag = jnp.zeros((8, tokens), F32)
    start = jnp.int32(0)
    for n in range(lengths.shape[0]):
        flag = jnp.where(lane == start - me * tokens, 1.0, flag)
        start = start + lengths[n]

    own = rate_out[...]
    guest = own
    for level in range(levels):
        rate_copies[level].wait()
        guest = jnp.where(jnp.full((8, tokens), partner, jnp.int32) == other(level), rate_in[level], guest)
    shift = slot - partner_slot + blocks
    for bit in range(blocks.bit_length() - 1):
        here = (jnp.full((8, tokens), shift, jnp.int32) >> bit) & 1
        guest = jnp.where(here == 1, pltpu.roll(guest, length << bit, 1), guest)
    rows = jnp.where(lane // length == jnp.full((8, tokens), slot, jnp.int32), guest, own)
    cum = jnp.where(sub == heads, flag, rows)
    step = 1
    while step < tokens:
        cum = cum + jnp.where(lane >= step, pltpu.roll(cum, step, 1), 0.0)
        step *= 2
    cum_s[...] = cum
    seg = cum[heads:heads + 1, :]
    seg_last = cum[heads:heads + 1, tokens - 1:tokens]
    cum_last = cum[:, tokens - 1:tokens]
    first8 = jnp.where(seg == 0.0, jnp.exp(-cum), 0.0)
    last8 = jnp.where(seg == seg_last, jnp.exp(cum - cum_last), 0.0)
    whole8 = jnp.where(seg_last == 0.0, jnp.exp(-cum_last), 0.0)
    w_out[...] = jnp.broadcast_to(whole8, (8, 128))
    w_copies = []
    for o in range(1, count):
        to = lax.rem(me + o, count)
        copy = remote(w_out, w_in.at[me], w_ss.at[o], w_rs.at[me], "dp", to)
        copy.start()
        w_copies.append(copy)
    w_in[me] = w_out[...]
    for h in range(heads):
        colb[h] = to_column(cum[h:h + 1, :], tokens)
        colb[heads + h] = to_column(first8[h:h + 1, :], tokens)
        colb[2 * heads + h] = to_column(last8[h:h + 1, :], tokens)
    segc[...] = to_column(seg, tokens)

    def make_decay(h, _):
        for tb in range(tiles):
            base = tb * (tb + 1) // 2 * TILE
            trow = pl.ds(tb * TILE, TILE)
            ct = twice(colb[h, trow, :])
            sc = twice(segc[trow, :])
            for sb in range(tb + 1):
                scol = pl.ds(sb * TILE, TILE)
                inside = cum_s[heads:heads + 1, scol] == sc
                if sb == tb:
                    r = lax.broadcasted_iota(jnp.int32, (TILE, TILE), 0)
                    c = lax.broadcasted_iota(jnp.int32, (TILE, TILE), 1)
                    inside = inside & (r >= c)
                value = jnp.exp(jnp.minimum(cum_s[pl.ds(h, 1), scol] - ct, 0.0)) * inv
                decay[h, :, base + sb * TILE:base + (sb + 1) * TILE] = jnp.where(inside, value, 0.0)
        return 0

    lax.fori_loop(0, heads, make_decay, 0)

    for level in range(levels):
        blk_copies[level].wait()
    for i, ref in enumerate((pk, pv, pq, pdy)):
        block = blk_out[i].astype(F32)
        for level in range(levels):
            match = jnp.full(block.shape, partner, jnp.int32) == other(level)
            block = jnp.where(match, blk_in[level, i].astype(F32), block)

        def put(b, _, ref=ref, block=block):
            at = pl.ds(pl.multiple_of(b * length, length), length)
            here = jnp.full(block.shape, slot, jnp.int32) == b
            ref[at, :] = jnp.where(here, block, ref[at, :].astype(F32)).astype(BF16)
            return 0

        lax.fori_loop(0, blocks, put, 0)

    def columns(h):
        return pl.ds(pl.multiple_of(h * HEAD_DIM, HEAD_DIM), HEAD_DIM)

    def state_rows(h):
        return pl.ds(pl.multiple_of(h * HEAD_DIM, HEAD_DIM), HEAD_DIM)

    def span_rows(j):
        return pl.ds(pl.multiple_of(j * span, span), span)

    def scatter(inbox, ss, rs):
        copies = []
        for o in range(1, count):
            to = lax.rem(me + o, count)
            copy = remote(st_out.at[span_rows(to)], inbox.at[me], ss.at[o], rs.at[me], "dp", to)
            copy.start()
            copies.append(copy)
        inbox[me] = st_out[span_rows(me), :]
        return copies

    def prefix(inbox, rs, outbox, home, ss2, rs2, reverse):
        for o in range(1, count):
            frm = lax.rem(me + count - o, count)
            remote(st_out.at[span_rows(0)], inbox.at[frm], ss2.at[o], rs.at[frm], "dp", frm).wait_recv()
        head = me * span // HEAD_DIM

        def one(turn, run):
            d = count - 1 - turn if reverse else turn
            outbox[d] = run.astype(BF16)
            w = w_in[d, pl.ds(head, 1), :]
            return twice(w) * run + inbox[d].astype(F32)

        lax.fori_loop(0, count, one, jnp.zeros((span, HEAD_DIM), F32))
        copies = []
        for o in range(1, count):
            to = lax.rem(me + o, count)
            copy = remote(outbox.at[to], home.at[span_rows(me)], ss2.at[o], rs2.at[me], "dp", to)
            copy.start()
            copies.append(copy)
        home[span_rows(me), :] = outbox[me]
        return copies

    def gather_wait(home, outbox, ss2, rs2):
        for o in range(1, count):
            frm = lax.rem(me + count - o, count)
            remote(outbox.at[0], home.at[span_rows(frm)], ss2.at[o], rs2.at[frm], "dp", frm).wait_recv()

    def local_state(h, _):
        gated = (pv[:, columns(h)].astype(F32) * twice(colb[2 * heads + h])).astype(BF16)
        st_out[state_rows(h), :] = dot_tn(pk[:, columns(h)], gated).astype(BF16)
        return 0

    lax.fori_loop(0, heads, local_state, 0)
    p1 = scatter(st_in, p1_ss, p1_rs)

    def forward(h, _):
        cols = columns(h)
        for tb in range(tiles):
            n = (tb + 1) * TILE
            base = tb * (tb + 1) // 2 * TILE
            trow = pl.ds(tb * TILE, TILE)
            scores = dot_nt(pq[trow, cols], pk[0:n, cols])
            w = (scores * decay[h, :, base:base + n]).astype(BF16)
            wts[h, trow, 0:n] = w
            ret[trow, cols] = dot_nn(w, pv[0:n, cols])
        return 0

    half = heads // 2
    lax.fori_loop(0, half, forward, 0)
    for o in range(1, count):
        w_copies[o - 1].wait_send()
        frm = lax.rem(me + count - o, count)
        remote(w_out, w_in.at[frm], w_ss.at[o], w_rs.at[frm], "dp", frm).wait_recv()
    p2 = prefix(st_in, p1_rs, st_ret, carry, p2_ss, p2_rs, False)
    lax.fori_loop(half, heads, forward, 0)
    gather_wait(carry, st_ret, p2_ss, p2_rs)

    def cross(h, sums):
        cols = columns(h)
        part = dot_nn(pq[:, cols], carry[state_rows(h), :])
        r = ret[:, cols] + part * (twice(colb[heads + h]) * inv)
        ret[:, cols] = r
        s = gain[:, cols] * pdy[:, cols].astype(F32)
        sq = r * r
        sr = s * r
        return (sums[0] + sq[:, 0:128] + sq[:, 128:256], sums[1] + sr[:, 0:128] + sr[:, 128:256])

    zero = jnp.zeros((tokens, 128), F32)
    sums = lax.fori_loop(0, heads, cross, (zero, zero))
    sq_row = jnp.sum(jnp.transpose(sums[0]), axis=0, keepdims=True)
    in_row = jnp.sum(jnp.transpose(sums[1]), axis=0, keepdims=True)
    hs_out[...] = jnp.where(sub == 0, sq_row, in_row)
    h_copies = []
    for o in range(1, hcount):
        to = lax.rem(hme + o, hcount)
        copy = remote(hs_out, hs_in.at[hme], hs_ss.at[o], hs_rs.at[hme], "head", to)
        copy.start()
        h_copies.append(copy)
    both = hs_out[...]
    for o in range(1, hcount):
        frm = lax.rem(hme + hcount - o, hcount)
        remote(hs_out, hs_in.at[frm], hs_ss.at[o], hs_rs.at[frm], "head", frm).wait_recv()
        both = both + hs_in[frm]
    for copy in p1:
        copy.wait_send()
    recip = lax.rsqrt(both[0:1, :] * (1.0 / FEATURES) + EPSILON)
    coef = recip * recip * recip * both[1:2, :] * (1.0 / FEATURES)
    hs_cols = (to_column(recip, tokens), to_column(coef, tokens))
    segc[...] = hs_cols[0]
    dkin[:, 0:128] = hs_cols[1]

    def back_state(h, _):
        cols = columns(h)
        s = gain[:, cols] * pdy[:, cols].astype(F32)
        g = (twice(segc[...]) * s - twice(dkin[:, 0:128]) * ret[:, cols]).astype(BF16)
        grad[:, cols] = g
        gated = (g.astype(F32) * twice(colb[heads + h])).astype(BF16)
        st_out[state_rows(h), :] = (dot_tn(pq[:, cols], gated) * inv).astype(BF16)
        return 0

    lax.fori_loop(0, heads, back_state, 0)
    b1 = scatter(bk_in, b1_ss, b1_rs)

    def backward(h, _):
        cols = columns(h)
        for tb in range(tiles):
            n = (tb + 1) * TILE
            base = tb * (tb + 1) // 2 * TILE
            trow = pl.ds(tb * TILE, TILE)
            g = grad[trow, cols]
            scores = dot_nt(g, pv[0:n, cols])
            w = (scores * decay[h, :, base:base + n]).astype(BF16)
            gw[trow, 0:n] = w
            part = dot_nt(g, carry[state_rows(h), :])
            fc = twice(colb[heads + h, trow, :]) * inv
            pdy[trow, cols] = (dot_nn(w, pk[0:n, cols]) + fc * part).astype(BF16)
        for sb in range(tiles):
            lo = sb * TILE
            srow = pl.ds(lo, TILE)
            dkin[srow, cols] = dot_tn(gw[lo:, lo:lo + TILE], pq[lo:, cols])
            ret[srow, cols] = dot_tn(wts[h, lo:, lo:lo + TILE], grad[lo:, cols])
        return 0

    lax.fori_loop(0, half, backward, 0)
    b2 = prefix(bk_in, b1_rs, bk_ret, cback, b2_ss, b2_rs, True)
    lax.fori_loop(half, heads, backward, 0)
    gather_wait(cback, bk_ret, b2_ss, b2_rs)

    def finish(h, _):
        cols = columns(h)
        lc = twice(colb[2 * heads + h])
        state = cback[state_rows(h), :]
        k = pk[:, cols]
        dk = dkin[:, cols] + lc * dot_nt(pv[:, cols], state)
        dv = ret[:, cols] + lc * dot_nn(k, state)
        pk[:, cols] = dk.astype(BF16)
        pv[:, cols] = dv.astype(BF16)
        return 0

    lax.fori_loop(0, heads, finish, 0)
    for i, ref in enumerate((pdy, pk, pv)):
        lv_out[i] = pick(ref)
    lv_copies = []
    for level in range(levels):
        copy = remote(lv_out, lv_in.at[level], lv_ss.at[level], lv_rs.at[level], "dp", other(level))
        copy.start()
        lv_copies.append(copy)
    stores = []
    for i, (src, dst) in enumerate(((pdy, dq_hbm), (pk, dk_hbm), (pv, dv_hbm))):
        copy = pltpu.make_async_copy(src, dst, out_sem.at[i])
        copy.start()
        stores.append(copy)
    for copy in p2 + b1 + b2 + h_copies:
        copy.wait_send()
    for copy in lv_copies:
        copy.wait()
    for i in range(3):
        block = lv_out[i].astype(F32)
        for level in range(levels):
            match = jnp.full(block.shape, partner, jnp.int32) == other(level)
            block = jnp.where(match, lv_in[level, i].astype(F32), block)
        guest_out[i] = block.astype(BF16)
    for copy in stores:
        copy.wait()


def place_kernel(chunk, slot, guest, dq, dk, dv, oq, ok, ov):
    oq[...] = dq[...]
    ok[...] = dk[...]
    ov[...] = dv[...]
    first = pl.program_id(0) * chunk
    at = slot[0] * BLOCK_LEN - first

    @pl.when((at >= 0) & (at < chunk))
    def _():
        rows = pl.ds(pl.multiple_of(at, BLOCK_LEN), BLOCK_LEN)
        oq[rows, :] = guest[0]
        ok[rows, :] = guest[1]
        ov[rows, :] = guest[2]


def local(count, hcount, queries, keys, values, out_grad, norm_gain, table, index, lengths, partners, slots):
    tokens, width = queries.shape
    heads = table.shape[0]
    tiles = tokens // TILE
    levels = count.bit_length() - 1
    span = heads * HEAD_DIM // count
    smem = pl.BlockSpec(memory_space=pltpu.SMEM)
    vmem = pl.BlockSpec(memory_space=pltpu.VMEM)
    any_ = pl.BlockSpec(memory_space=pl.ANY)
    full = jax.ShapeDtypeStruct((tokens, width), BF16)
    V = pltpu.VMEM
    D = pltpu.SemaphoreType.DMA
    state = V((heads * HEAD_DIM, HEAD_DIM), BF16)
    part = V((count, span, HEAD_DIM), BF16)
    dq, dk, dv, guest = pl.pallas_call(
        functools.partial(main_kernel, count, hcount, heads, tokens),
        out_shape=(full, full, full, jax.ShapeDtypeStruct((3, BLOCK_LEN, width), BF16)),
        in_specs=[smem, smem, smem, vmem, vmem, vmem, any_, any_, any_, any_],
        out_specs=(any_, any_, any_, vmem),
        scratch_shapes=[
            V((tokens, width), BF16), V((tokens, width), BF16), V((tokens, width), BF16), V((tokens, width), BF16),
            V((heads, tokens, tokens), BF16),
            V((heads, TILE, tiles * (tiles + 1) // 2 * TILE), F32),
            V((tokens, tokens), BF16),
            V((tokens, width), F32), V((tokens, width), F32), V((tokens, width), BF16),
            V((3 * heads, tokens, 128), F32), V((tokens, 128), F32), V((8, tokens), F32),
            V((8, tokens), F32), V((levels, 8, tokens), F32),
            V((4, BLOCK_LEN, width), BF16), V((levels, 4, BLOCK_LEN, width), BF16),
            V((count, 8, 128), F32), V((8, 128), F32),
            state, part, part, state, part, part, state,
            V((8, tokens), F32), V((hcount, 8, tokens), F32),
            V((3, BLOCK_LEN, width), BF16), V((levels, 3, BLOCK_LEN, width), BF16),
            D((4,)), D((3,)), D((levels,)), D((levels,)), D((levels,)), D((levels,)),
            D((count,)), D((count,)), D((count,)), D((count,)), D((count,)), D((count,)),
            D((count,)), D((count,)), D((count,)), D((count,)),
            D((hcount,)), D((hcount,)), D((levels,)), D((levels,)),
        ],
        compiler_params=pltpu.CompilerParams(
            collective_id=0, has_side_effects=True, vmem_limit_bytes=60 * 1024 * 1024
        ),
    )(lengths, partners, slots, table, index, norm_gain.reshape(1, width), queries, keys, values, out_grad)

    slot = lax.dynamic_slice_in_dim(slots, lax.axis_index("dp"), 1, 0)
    chunk = 256
    block = pl.BlockSpec((chunk, width), lambda i: (i, 0))
    return pl.pallas_call(
        functools.partial(place_kernel, chunk),
        grid=(tokens // chunk,),
        out_shape=(full, full, full),
        in_specs=[smem, pl.BlockSpec((3, BLOCK_LEN, width), lambda i: (0, 0, 0)), block, block, block],
        out_specs=(block, block, block),
    )(slot, guest, dq, dk, dv)


def solution(mesh):
    placed = (
        P("dp", "head"), P("dp", "head"), P("dp", "head"), P("dp", "head"),
        P("head"), P("head", None), P("head", "dp"), P(), P(), P(),
    )
    return jax.shard_map(
        functools.partial(local, mesh.shape["dp"], mesh.shape["head"]),
        mesh=mesh,
        in_specs=placed,
        out_specs=(P("dp", "head"), P("dp", "head"), P("dp", "head")),
        check_vma=False,
    )
```

time: 442 us -> 109 us (0.25); the launches traced: 436 us -> 108 us
  waiting for transfers between devices: 205 us -> 0 us
  Pallas kernels: 0 us -> 106 us
  local copies, waits for them, and re-layouts: 64.6 us -> 1.31 us
  matrix products: 47 us -> 0 us
  blocking collectives: 37.1 us -> 0 us
  starting transfers between devices: 37 us -> 0 us
  other arithmetic: 25 us -> 0 us
  between operations: 19.1 us -> 0.64 us
    all_gather x2 -> x0, waiting for transfers between devices: 153 us -> none  [entering(): gathered = jax.tree.map(lambda a: lax.all_gather(a, axis), part)]
    pallas_call x0 -> x2, Pallas kernels: none -> 106 us  [the longest x1 98.9 us: local(): pl.pallas_call(functools.partial(main_kernel, count, hcount, heads, token...]
    ppermute x24 -> x0, waiting for transfers between devices: 52.2 us -> none  [partner_2(): return lax.ppermute(block, axis, route)]
    dot_general x48 -> x0, matrix products: 47 us -> none  [the longest x16 24.7 us: contract_last(): lax.dot_general(left, right, (((1,), (1,)), ((), ())), preferred_element_...]
    unnamed x107 -> x0, local copies, waits for them, and re-layouts: 43.3 us -> none
    ppermute x24 -> x0, starting transfers between devices: 37 us -> none  [partner_2(): return lax.ppermute(block, axis, route)]
    unnamed x1 -> x0, blocking collectives: 30.7 us -> none
    dynamic_update_slice x8 -> x0, local copies, waits for them, and re-layouts: 15.2 us -> none  [place_block(): lax.dynamic_update_slice_in_dim(array, block, block_id * block.shape[axis...]
  transfers between devices with their start and end apart: 26 -> 0, of which waited for: 10 -> 0; matrix products, arithmetic and copies ran while one was open for 15% -> 0% of each run, Pallas kernels for 0% -> 0%
where the time goes in v1:
time: 109 us; the launch traced here: 108 us
  Pallas kernels  106 us (97%)
  local copies, waits for them, and re-layouts  1.31 us (1%)
    pallas_call x1, Pallas kernels, local(): pl.pallas_call(functools.partial(main_kernel, count, hcount, heads, token...  98.9 us
    pallas_call x1, Pallas kernels, local(): pl.pallas_call(functools.partial(place_kernel, chunk), grid=(tokens // ch...  6.78 us

profile of v1, /device:TPU:0, one launch (start us, length us, event | category | flops | bytes accessed | tf_op | source)
XLA Modules:
  0.0 107.6 jit_solution(4480528781416583232)
XLA Ops:
  0.6 1.3 %dynamic_slice.3.slot = s32[1]{0:T(128)} dynamic-slice(s32[8]{0:T(128)} %slots.1, s32[]{:T(128)S(6)} %select_n.3), dynamic_slice_sizes={1} | dynamic-slice | bytes 12 | tf_op jit(solution)/shard_map/dynamic_slice | solution.py:443
  1.9 98.9 %shard_map.121 = (bf16[1024,1024]{1,0:T(8,128)(2,1)}, bf16[1024,1024]{1,0:T(8,128)(2,1)}, bf16[1024,1024]{1,0:T(8,128)(2,1)}, bf16[3,32,1024]{2,1,0:T(8,128)(2,1)}) custom-call(s32[6]{0:T(128)} %lengths.1, s32[8]{0:T(128)} %partners.1, s32[8]{0:T(128)} %slots.1, f32[4,8]{1,0:T(4,128)} %table.1, s32[4,1024]{1,0:T(4,128)} %index.1, f32[1,1024]{1,0:T(1,128)} %bitcast.1, ...), custom_call_target="tpu_custom_call" | custom-call | tf_op jit(solution)/shard_map/pallas_call | solution.py:415
  100.8 6.8 %shard_map.122 = (bf16[1024,1024]{1,0:T(8,128)(2,1)}, bf16[1024,1024]{1,0:T(8,128)(2,1)}, bf16[1024,1024]{1,0:T(8,128)(2,1)}) custom-call(s32[1]{0:T(128)} %dynamic_slice.3.slot, bf16[3,32,1024]{2,1,0:T(8,128)(2,1)} %get-tuple-element.7.guest, bf16[1024,1024]{1,0:T(8,128)(2,1)} %get-tuple-element.8.dq, bf16[1024,1024]{1,0:T(8,128)(2,1)} %get-tuple-element.9.dk, ...), custom_call_target="tpu_custom_call" | custom-call | tf_op jit(solution)/shard_map/pallas_call | solution.py:446

commit v2 on v1

--- a/solution.py
+++ b/solution.py
@@ -42,17 +42,22 @@
     lengths, partners, slots, table, index, gain, q_hbm, k_hbm, v_hbm, dy_hbm,
     dq_hbm, dk_hbm, dv_hbm, guest_out,
     pq, pk, pv, pdy, wts, decay, gw, ret, dkin, grad, colb, segc, cum_s,
-    rate_out, rate_in, blk_out, blk_in, w_in, w_out,
-    st_out, st_in, st_ret, carry, bk_in, bk_ret, cback,
+    sel, unsel, rate_out, rate_in, blk_out, blk_in, w_in, w_out,
+    st_out, st_in, st_ret, carry, bk_in, bk_ret, cback, mid_out, mid_in,
     hs_out, hs_in, lv_out, lv_in,
     in_sem, out_sem, rate_ss, rate_rs, blk_ss, blk_rs, w_ss, w_rs,
-    p1_ss, p1_rs, p2_ss, p2_rs, b1_ss, b1_rs, b2_ss, b2_rs, hs_ss, hs_rs, lv_ss, lv_rs,
+    p1_ss, p1_rs, p2_ss, p2_rs, b1_ss, b1_rs, b2_ss, b2_rs, mid_ss, mid_rs, hs_ss, hs_rs, lv_ss, lv_rs,
 ):
     me = lax.axis_index("dp")
     hme = lax.axis_index("head")
     levels = count.bit_length() - 1
     length = BLOCK_LEN
-    span = heads * HEAD_DIM // count
+    group = count // 2
+    side = me // group
+    base_row = side * group
+    pos = me - base_row
+    mate = me + group - 2 * group * side
+    span = heads * HEAD_DIM // group
     tiles = tokens // TILE
     width = heads * HEAD_DIM
     inv = 1.0 / HEAD_DIM
@@ -101,23 +106,57 @@
 
     blocks = tokens // length
 
+    chosen = lax.broadcasted_iota(jnp.int32, (tokens, 128), 0) // length == jnp.full((tokens, 128), slot, jnp.int32)
+    sel[...] = jnp.where(chosen, 1.0, 0.0).astype(BF16)
+    unsel[...] = jnp.where(chosen, 0.0, 1.0).astype(BF16)
+
+    def widen(mask):
+        return jnp.concatenate([mask] * (width // 128), axis=1)
+
     def pick(ref):
-        slot_of = jnp.full((length, width), slot, jnp.int32)
-
         def one(b, acc):
-            part = ref[pl.ds(pl.multiple_of(b * length, length), length), :].astype(F32)
-            return jnp.where(slot_of == b, part, acc)
-
-        return lax.fori_loop(0, blocks, one, jnp.zeros((length, width), F32)).astype(BF16)
-
-    for i, ref in enumerate((pk, pv, pq, pdy)):
+            at = pl.ds(pl.multiple_of(b * length, length), length)
+            return acc + ref[at, :] * widen(sel[at, :])
+
+        return lax.fori_loop(0, blocks, one, jnp.zeros((length, width), BF16))
+
+    def to_partners(out, inbox, ss, rs, first):
+        copies = []
+        for level in range(levels):
+            copy = remote(out, inbox(level), ss.at[first + level], rs.at[first + level], "dp", other(level))
+            copy.start()
+            copies.append(copy)
+        return copies
+
+    def guest_of(own_block, inbox):
+        block = own_block.astype(F32)
+        for level in range(levels):
+            match = jnp.full(block.shape, partner, jnp.int32) == other(level)
+            block = jnp.where(match, inbox(level).astype(F32), block)
+        return block.astype(BF16)
+
+    def put(ref, i):
+        block = guest_of(blk_out[i], lambda level: blk_in[level, i])
+
+        def one(b, _):
+            at = pl.ds(pl.multiple_of(b * length, length), length)
+            ref[at, :] = ref[at, :] * widen(unsel[at, :]) + block * widen(sel[at, :])
+            return 0
+
+        lax.fori_loop(0, blocks, one, 0)
+
+    packed = (pk, pv, pq, pdy)
+
+    def load_and_pick(i):
         loads[i].wait()
-        blk_out[i] = pick(ref)
-    blk_copies = []
-    for level in range(levels):
-        copy = remote(blk_out, blk_in.at[level], blk_ss.at[level], blk_rs.at[level], "dp", other(level))
-        copy.start()
-        blk_copies.append(copy)
+        blk_out[i] = pick(packed[i])
+
+    load_and_pick(0)
+    load_and_pick(1)
+    kv_copies = to_partners(blk_out.at[0:2], lambda level: blk_in.at[level, 0:2], blk_ss, blk_rs, 0)
+    load_and_pick(2)
+    q_copies = to_partners(blk_out.at[2], lambda level: blk_in.at[level, 2], blk_ss, blk_rs, levels)
+    load_and_pick(3)
 
     lane = lax.broadcasted_iota(jnp.int32, (8, tokens), 1)
     sub = lax.broadcasted_iota(jnp.int32, (8, tokens), 0)
@@ -182,21 +221,10 @@
 
     lax.fori_loop(0, heads, make_decay, 0)
 
-    for level in range(levels):
-        blk_copies[level].wait()
-    for i, ref in enumerate((pk, pv, pq, pdy)):
-        block = blk_out[i].astype(F32)
-        for level in range(levels):
-            match = jnp.full(block.shape, partner, jnp.int32) == other(level)
-            block = jnp.where(match, blk_in[level, i].astype(F32), block)
-
-        def put(b, _, ref=ref, block=block):
-            at = pl.ds(pl.multiple_of(b * length, length), length)
-            here = jnp.full(block.shape, slot, jnp.int32) == b
-            ref[at, :] = jnp.where(here, block, ref[at, :].astype(F32)).astype(BF16)
-            return 0
-
-        lax.fori_loop(0, blocks, put, 0)
+    for copy in kv_copies:
+        copy.wait()
+    put(pk, 0)
+    put(pv, 1)
 
     def columns(h):
         return pl.ds(pl.multiple_of(h * HEAD_DIM, HEAD_DIM), HEAD_DIM)
@@ -209,40 +237,53 @@
 
     def scatter(inbox, ss, rs):
         copies = []
-        for o in range(1, count):
-            to = lax.rem(me + o, count)
-            copy = remote(st_out.at[span_rows(to)], inbox.at[me], ss.at[o], rs.at[me], "dp", to)
+        for o in range(1, group):
+            to = lax.rem(pos + o, group)
+            copy = remote(st_out.at[span_rows(to)], inbox.at[pos], ss.at[o], rs.at[pos], "dp", base_row + to)
             copy.start()
             copies.append(copy)
-        inbox[me] = st_out[span_rows(me), :]
+        inbox[pos] = st_out[span_rows(pos), :]
         return copies
 
-    def prefix(inbox, rs, outbox, home, ss2, rs2, reverse):
-        for o in range(1, count):
-            frm = lax.rem(me + count - o, count)
-            remote(st_out.at[span_rows(0)], inbox.at[frm], ss2.at[o], rs.at[frm], "dp", frm).wait_recv()
-        head = me * span // HEAD_DIM
-
+    head_of_span = pos * span // HEAD_DIM
+
+    def fold(inbox, run, reverse, outbox):
         def one(turn, run):
-            d = count - 1 - turn if reverse else turn
-            outbox[d] = run.astype(BF16)
-            w = w_in[d, pl.ds(head, 1), :]
+            d = group - 1 - turn if reverse else turn
+            if outbox is not None:
+                outbox[d] = run.astype(BF16)
+            w = w_in[base_row + d, pl.ds(head_of_span, 1), :]
             return twice(w) * run + inbox[d].astype(F32)
 
-        lax.fori_loop(0, count, one, jnp.zeros((span, HEAD_DIM), F32))
+        return lax.fori_loop(0, group, one, run)
+
+    def across(inbox, rs, ss, which, reverse):
+        for o in range(1, group):
+            frm = lax.rem(pos + group - o, group)
+            remote(st_out.at[span_rows(0)], inbox.at[frm], ss.at[o], rs.at[frm], "dp", base_row + frm).wait_recv()
+        mid_out[which] = fold(inbox, jnp.zeros((span, HEAD_DIM), F32), reverse, None).astype(BF16)
+        copy = remote(mid_out.at[which], mid_in.at[which], mid_ss.at[which], mid_rs.at[which], "dp", mate)
+        copy.start()
+        return copy
+
+    def prefix(inbox, outbox, home, ss2, rs2, which, copy, reverse):
+        copy.wait_recv()
+        behind = jnp.full((span, HEAD_DIM), side, jnp.int32) == (0 if reverse else 1)
+        run = jnp.where(behind, mid_in[which].astype(F32), 0.0)
+        fold(inbox, run, reverse, outbox)
         copies = []
-        for o in range(1, count):
-            to = lax.rem(me + o, count)
-            copy = remote(outbox.at[to], home.at[span_rows(me)], ss2.at[o], rs2.at[me], "dp", to)
-            copy.start()
-            copies.append(copy)
-        home[span_rows(me), :] = outbox[me]
+        for o in range(1, group):
+            to = lax.rem(pos + o, group)
+            out = remote(outbox.at[to], home.at[span_rows(pos)], ss2.at[o], rs2.at[pos], "dp", base_row + to)
+            out.start()
+            copies.append(out)
+        home[span_rows(pos), :] = outbox[pos]
         return copies
 
     def gather_wait(home, outbox, ss2, rs2):
-        for o in range(1, count):
-            frm = lax.rem(me + count - o, count)
-            remote(outbox.at[0], home.at[span_rows(frm)], ss2.at[o], rs2.at[frm], "dp", frm).wait_recv()
+        for o in range(1, group):
+            frm = lax.rem(pos + group - o, group)
+            remote(outbox.at[0], home.at[span_rows(frm)], ss2.at[o], rs2.at[frm], "dp", base_row + frm).wait_recv()
 
     def local_state(h, _):
         gated = (pv[:, columns(h)].astype(F32) * twice(colb[2 * heads + h])).astype(BF16)
@@ -251,6 +292,10 @@
 
     lax.fori_loop(0, heads, local_state, 0)
     p1 = scatter(st_in, p1_ss, p1_rs)
+    dy_copies = to_partners(blk_out.at[3], lambda level: blk_in.at[level, 3], blk_ss, blk_rs, 2 * levels)
+    for copy in q_copies:
+        copy.wait()
+    put(pq, 2)
 
     def forward(h, _):
         cols = columns(h)
@@ -264,14 +309,19 @@
             ret[trow, cols] = dot_nn(w, pv[0:n, cols])
         return 0
 
-    half = heads // 2
-    lax.fori_loop(0, half, forward, 0)
+    cut_a, cut_b = heads // 2, 3 * heads // 4
+    lax.fori_loop(0, cut_a, forward, 0)
     for o in range(1, count):
         w_copies[o - 1].wait_send()
         frm = lax.rem(me + count - o, count)
         remote(w_out, w_in.at[frm], w_ss.at[o], w_rs.at[frm], "dp", frm).wait_recv()
-    p2 = prefix(st_in, p1_rs, st_ret, carry, p2_ss, p2_rs, False)
-    lax.fori_loop(half, heads, forward, 0)
+    mid = across(st_in, p1_rs, p1_ss, 0, False)
+    lax.fori_loop(cut_a, cut_b, forward, 0)
+    p2 = prefix(st_in, st_ret, carry, p2_ss, p2_rs, 0, mid, False)
+    lax.fori_loop(cut_b, heads, forward, 0)
+    for copy in dy_copies:
+        copy.wait()
+    put(pdy, 3)
     gather_wait(carry, st_ret, p2_ss, p2_rs)
 
     def cross(h, sums):
@@ -340,9 +390,15 @@
             ret[srow, cols] = dot_tn(wts[h, lo:, lo:lo + TILE], grad[lo:, cols])
         return 0
 
-    lax.fori_loop(0, half, backward, 0)
-    b2 = prefix(bk_in, b1_rs, bk_ret, cback, b2_ss, b2_rs, True)
-    lax.fori_loop(half, heads, backward, 0)
+    lax.fori_loop(0, cut_a, backward, 0)
+    back_mid = across(bk_in, b1_rs, b1_ss, 1, True)
+    lax.fori_loop(cut_a, cut_b, backward, 0)
+    b2 = prefix(bk_in, bk_ret, cback, b2_ss, b2_rs, 1, back_mid, True)
+    lax.fori_loop(cut_b, heads, backward, 0)
+    lv_out[0] = pick(pdy)
+    lv_copies = to_partners(lv_out.at[0], lambda level: lv_in.at[level, 0], lv_ss, lv_rs, 0)
+    stores = [pltpu.make_async_copy(pdy, dq_hbm, out_sem.at[0])]
+    stores[0].start()
     gather_wait(cback, bk_ret, b2_ss, b2_rs)
 
     def finish(h, _):
@@ -357,38 +413,29 @@
         return 0
 
     lax.fori_loop(0, heads, finish, 0)
-    for i, ref in enumerate((pdy, pk, pv)):
-        lv_out[i] = pick(ref)
-    lv_copies = []
-    for level in range(levels):
-        copy = remote(lv_out, lv_in.at[level], lv_ss.at[level], lv_rs.at[level], "dp", other(level))
-        copy.start()
-        lv_copies.append(copy)
-    stores = []
-    for i, (src, dst) in enumerate(((pdy, dq_hbm), (pk, dk_hbm), (pv, dv_hbm))):
-        copy = pltpu.make_async_copy(src, dst, out_sem.at[i])
+    lv_out[1] = pick(pk)
+    lv_out[2] = pick(pv)
+    lv_copies += to_partners(lv_out.at[1:3], lambda level: lv_in.at[level, 1:3], lv_ss, lv_rs, levels)
+    for i, (src, dst) in enumerate(((pk, dk_hbm), (pv, dv_hbm))):
+        copy = pltpu.make_async_copy(src, dst, out_sem.at[i + 1])
         copy.start()
         stores.append(copy)
-    for copy in p2 + b1 + b2 + h_copies:
+    for copy in p2 + b1 + b2 + h_copies + [mid, back_mid]:
         copy.wait_send()
     for copy in lv_copies:
         copy.wait()
     for i in range(3):
-        block = lv_out[i].astype(F32)
-        for level in range(levels):
-            match = jnp.full(block.shape, partner, jnp.int32) == other(level)
-            block = jnp.where(match, lv_in[level, i].astype(F32), block)
-        guest_out[i] = block.astype(BF16)
+        guest_out[i] = guest_of(lv_out[i], lambda level: lv_in[level, i])
     for copy in stores:
         copy.wait()
 
 
-def place_kernel(chunk, slot, guest, dq, dk, dv, oq, ok, ov):
+def place_kernel(chunk, slots, guest, dq, dk, dv, oq, ok, ov):
     oq[...] = dq[...]
     ok[...] = dk[...]
     ov[...] = dv[...]
     first = pl.program_id(0) * chunk
-    at = slot[0] * BLOCK_LEN - first
+    at = slots[lax.axis_index("dp")] * BLOCK_LEN - first
 
     @pl.when((at >= 0) & (at < chunk))
     def _():
@@ -403,7 +450,8 @@
     heads = table.shape[0]
     tiles = tokens // TILE
     levels = count.bit_length() - 1
-    span = heads * HEAD_DIM // count
+    group = count // 2
+    span = heads * HEAD_DIM // group
     smem = pl.BlockSpec(memory_space=pltpu.SMEM)
     vmem = pl.BlockSpec(memory_space=pltpu.VMEM)
     any_ = pl.BlockSpec(memory_space=pl.ANY)
@@ -411,7 +459,7 @@
     V = pltpu.VMEM
     D = pltpu.SemaphoreType.DMA
     state = V((heads * HEAD_DIM, HEAD_DIM), BF16)
-    part = V((count, span, HEAD_DIM), BF16)
+    part = V((group, span, HEAD_DIM), BF16)
     dq, dk, dv, guest = pl.pallas_call(
         functools.partial(main_kernel, count, hcount, heads, tokens),
         out_shape=(full, full, full, jax.ShapeDtypeStruct((3, BLOCK_LEN, width), BF16)),
@@ -424,24 +472,25 @@
             V((tokens, tokens), BF16),
             V((tokens, width), F32), V((tokens, width), F32), V((tokens, width), BF16),
             V((3 * heads, tokens, 128), F32), V((tokens, 128), F32), V((8, tokens), F32),
+            V((tokens, 128), BF16), V((tokens, 128), BF16),
             V((8, tokens), F32), V((levels, 8, tokens), F32),
             V((4, BLOCK_LEN, width), BF16), V((levels, 4, BLOCK_LEN, width), BF16),
             V((count, 8, 128), F32), V((8, 128), F32),
             state, part, part, state, part, part, state,
+            V((2, span, HEAD_DIM), BF16), V((2, span, HEAD_DIM), BF16),
             V((8, tokens), F32), V((hcount, 8, tokens), F32),
             V((3, BLOCK_LEN, width), BF16), V((levels, 3, BLOCK_LEN, width), BF16),
-            D((4,)), D((3,)), D((levels,)), D((levels,)), D((levels,)), D((levels,)),
-            D((count,)), D((count,)), D((count,)), D((count,)), D((count,)), D((count,)),
-            D((count,)), D((count,)), D((count,)), D((count,)),
-            D((hcount,)), D((hcount,)), D((levels,)), D((levels,)),
+            D((4,)), D((3,)), D((levels,)), D((levels,)), D((3 * levels,)), D((3 * levels,)),
+            D((count,)), D((count,)), D((group,)), D((group,)), D((group,)), D((group,)),
+            D((group,)), D((group,)), D((group,)), D((group,)), D((2,)), D((2,)),
+            D((hcount,)), D((hcount,)), D((2 * levels,)), D((2 * levels,)),
         ],
         compiler_params=pltpu.CompilerParams(
             collective_id=0, has_side_effects=True, vmem_limit_bytes=60 * 1024 * 1024
         ),
     )(lengths, partners, slots, table, index, norm_gain.reshape(1, width), queries, keys, values, out_grad)
 
-    slot = lax.dynamic_slice_in_dim(slots, lax.axis_index("dp"), 1, 0)
-    chunk = 256
+    chunk = 128
     block = pl.BlockSpec((chunk, width), lambda i: (i, 0))
     return pl.pallas_call(
         functools.partial(place_kernel, chunk),
@@ -449,7 +498,7 @@
         out_shape=(full, full, full),
         in_specs=[smem, pl.BlockSpec((3, BLOCK_LEN, width), lambda i: (0, 0, 0)), block, block, block],
         out_specs=(block, block, block),
-    )(slot, guest, dq, dk, dv)
+    )(slots, guest, dq, dk, dv)
 
 
 def solution(mesh):

time: 109 us -> 91.8 us (0.84)
  Pallas kernels: 106 us -> 90.1 us
  local copies, waits for them, and re-layouts: 1.31 us -> 0 us
    pallas_call x1, Pallas kernels: 98.9 us -> 82.1 us  [local(): pl.pallas_call(functools.partial(main_kernel, count, hcount, heads, token...]
    dynamic_slice x1 -> x0, local copies, waits for them, and re-layouts: 1.31 us -> none  [local(): slot = lax.dynamic_slice_in_dim(slots, lax.axis_index('dp'), 1, 0)]
    pallas_call x1, Pallas kernels: 6.78 us -> 7.96 us  [local(): pl.pallas_call(functools.partial(place_kernel, chunk), grid=(tokens // ch...]
where the time goes in v2:
time: 91.8 us; the launch traced here: 90.7 us
  Pallas kernels  90.1 us (98%)
    pallas_call x1, Pallas kernels, local(): pl.pallas_call(functools.partial(main_kernel, count, hcount, heads, token...  82.1 us
    pallas_call x1, Pallas kernels, local(): pl.pallas_call(functools.partial(place_kernel, chunk), grid=(tokens // ch...  7.96 us

profile of v2, /device:TPU:0, one launch (start us, length us, event | category | flops | bytes accessed | tf_op | source)
XLA Modules:
  0.0 90.7 jit_solution(2039565200679307007)
XLA Ops:
  0.6 82.1 %shard_map.121 = (bf16[1024,1024]{1,0:T(8,128)(2,1)}, bf16[1024,1024]{1,0:T(8,128)(2,1)}, bf16[1024,1024]{1,0:T(8,128)(2,1)}, bf16[3,32,1024]{2,1,0:T(8,128)(2,1)}) custom-call(s32[6]{0:T(128)} %lengths.1, s32[8]{0:T(128)} %partners.1, s32[8]{0:T(128)} %slots.3, f32[4,8]{1,0:T(4,128)} %table.1, s32[4,1024]{1,0:T(4,128)} %index.1, f32[1,1024]{1,0:T(1,128)} %bitcast.1, ...), custom_call_target="tpu_custom_call" | custom-call | tf_op jit(solution)/shard_map/pallas_call | solution.py:463
  82.7 8.0 %shard_map.122 = (bf16[1024,1024]{1,0:T(8,128)(2,1)}, bf16[1024,1024]{1,0:T(8,128)(2,1)}, bf16[1024,1024]{1,0:T(8,128)(2,1)}) custom-call(s32[8]{0:T(128)} %slots.3, bf16[3,32,1024]{2,1,0:T(8,128)(2,1)} %get-tuple-element.7.guest, bf16[1024,1024]{1,0:T(8,128)(2,1)} %get-tuple-element.8.dq, bf16[1024,1024]{1,0:T(8,128)(2,1)} %get-tuple-element.9.dk, ...), custom_call_target="tpu_custom_call" | custom-call | tf_op jit(solution)/shard_map/pallas_call | solution.py:495
